TPU v7x, 256 devices: a whole 4x4x8 slice. The times are simulated.
256 devices in a mesh: dp: 8 (over y, core), tm: 32 (over z, x).
Axes of the slice: x: 4, y: 4, z: 8, core: 2. Of those that a mesh axis runs over, the one named last changes fastest.
Arguments:
- frames: bfloat16 [65536, 1536], P(('dp', 'tm')), may hold values from -28 to 28, as said below
- seg: int32 [8, 8192], P('dp'), may hold values from 0 to 3, never falling along the last dimension, each value on 1 to 4096 neighbouring positions
- look_back: int32 [8, 32], P('dp'), may hold values 0 or 1
- w_dw: float32 [5, 1536], replicated, may hold values from -2.5 to 2.5
- w_qkv: bfloat16 [1536, 4608], P(None, 'dp'), may hold values from -0.15625 to 0.15625
- w_o: bfloat16 [1536, 1536], replicated, may hold values from -1.5 to 1.5
- cotangent: bfloat16 [65536, 1536], P(('dp', 'tm')), may hold values from -1 to 1
Outputs:
- mixed: bfloat16 [65536, 1536], P(('dp', 'tm'))
- weight_grad: float32 [1536, 1536], P('tm', 'dp')
Inputs may be any that keep to these rules, and one draw needn't show every extreme that they name: Float features; a few short runs of frames may be several times larger than the rest. `seg`: recording numbers never fall along a replica's frames; each recording has 1 to 4096 frames, one exactly 4096.
All inputs are finite; a program needn't handle non-finite values. No bound on the sum of `look_back` on one device may be relied on, other than what follows from the above.
Results may differ from a plain program's by a relative error of at most 0.012.
The roundings to bfloat16 on the way count: a program that leaves them out, or rounds other values in their place, can miss the bound.
Values may be sent and summed in bfloat16 or wider, within the bound.
A program may use at most 128 MiB of HBM per device.

v0:
```python
import math
import jax
import jax.numpy as jnp
from jax import lax
from jax.sharding import PartitionSpec as P

KER = 5
HEADS = 16
HALF = KER // 2


def conv_silu(rows_in, seg_in, w_dw):
    count = rows_in.shape[0] - 2 * HALF
    own = seg_in[HALF : HALF + count]
    total = jnp.zeros((count, rows_in.shape[1]), jnp.float32)
    for offset in range(KER):
        same = (seg_in[offset : offset + count] == own).astype(jnp.float32)
        total = (
            total
            + w_dw[offset] * rows_in[offset : offset + count].astype(jnp.float32) * same[:, None]
        )
    return jax.nn.silu(total).astype(jnp.bfloat16)


def local(frames, seg, look_back, w_dw, w_qkv, w_o, cotangent):
    rows, width = frames.shape
    count = lax.axis_size("tm")
    me = lax.axis_index("tm")
    weights = lax.all_gather(w_qkv, "dp", axis=1, tiled=True)
    before = lax.ppermute(frames, "tm", [(i, i + 1) for i in range(count - 1)])
    far = lax.ppermute(frames[-HALF:], "tm", [(i, i + 2) for i in range(count - 2)])
    after = lax.ppermute(frames[:HALF], "tm", [(i + 1, i) for i in range(count - 1)])
    stack = jnp.concatenate([far, before, frames, after], 0)
    seg_padded = jnp.pad(seg[0], (rows + HALF, HALF), constant_values=-1)
    local_seg = lax.dynamic_slice_in_dim(seg_padded, me * rows, 2 * rows + 2 * HALF, 0)
    activ = conv_silu(stack, local_seg, w_dw)
    qkv = jnp.dot(activ[rows:], weights, preferred_element_type=jnp.float32).astype(jnp.bfloat16)
    kv_before = jnp.dot(
        activ[:rows], weights[:, width:], preferred_element_type=jnp.float32
    ).astype(jnp.bfloat16)
    head_dim = width // HEADS
    queries = qkv[:, :width].reshape(rows, HEADS, head_dim)
    kv = jnp.concatenate([kv_before, qkv[:, width:]], 0).reshape(2 * rows, 2, HEADS, head_dim)
    scores = jnp.einsum("qhd,khd->hqk", queries, kv[:, 0], preferred_element_type=jnp.float32) * (
        1.0 / math.sqrt(head_dim)
    )
    seg_pair = local_seg[HALF : HALF + 2 * rows]
    same_rec = seg_pair[rows:][:, None] == seg_pair[None, :]
    look = lax.dynamic_slice_in_dim(look_back[0], me, 1, 0)[0] == 1
    allowed = same_rec & ((jnp.arange(2 * rows) >= rows) | look)[None, :]
    scores = jnp.where(allowed[None], scores, -1e30)
    raw = jnp.exp(scores - jnp.max(scores, axis=-1, keepdims=True))
    probs = (raw / jnp.sum(raw, axis=-1, keepdims=True)).astype(jnp.bfloat16)
    attn = jnp.einsum("hqk,khv->qhv", probs, kv[:, 1], preferred_element_type=jnp.float32)
    attn = attn.astype(jnp.bfloat16).reshape(rows, width)
    mixed = jnp.dot(attn, w_o, preferred_element_type=jnp.float32).astype(jnp.bfloat16)
    grad_term = lax.dot_general(
        attn, cotangent, (((0,), (0,)), ((), ())), preferred_element_type=jnp.float32
    )
    col_share = lax.psum_scatter(grad_term, "dp", scatter_dimension=1, tiled=True)
    weight_grad = lax.psum_scatter(col_share, "tm", scatter_dimension=0, tiled=True)
    return (mixed, weight_grad)


def solution(mesh):
    placed = (
        P(("dp", "tm"), None),
        P("dp", None),
        P("dp", None),
        P(),
        P(None, "dp"),
        P(),
        P(("dp", "tm"), None),
    )
    return jax.shard_map(
        local,
        mesh=mesh,
        in_specs=placed,
        out_specs=(P(("dp", "tm"), None), P("tm", "dp")),
        check_vma=False,
    )
```

profile of v0, /device:TPU:8, one launch (start us, length us, event | category | flops | bytes accessed | tf_op | source)
XLA Modules:
  0.0 419.2 jit_solution(788652810859067581)
XLA Ops:
  7.2 0.7 all-gather.2.cloned.1.call-update
  8.0 3.4 collective-permute-start.1
  11.4 0.8 fusion.22
  12.2 4.6 %collective-permute-start = (bf16[2,1536]{1,0:T(2,128)(2,1)S(1)}, bf16[2,1536]{1,0:T(2,128)(2,1)S(1)}, u32[]{:S(2)}, u32[]{:S(2)}) collective-permute-start(bf16[2,1536]{1,0:T(2,128)(2,1)S(1)} %get-tuple-element.13), channel_id=1, source_target_pairs={{0,2},{1,3},{2,4},{3,5},{4,6},{5,7},{6,8},{7,9},{8,10},{9,11},{10,... | collective-permute-start | bytes 18440 | tf_op jit(solution)/shard_map/ppermute | solution.py:31
  16.8 1.3 collective-permute-start.2
  18.1 0.8 pad_dynamic-slice_fusion
  19.1 1.2 fusion.23
  20.9 1.1 slice_reduce_fusion.4
  22.3 6.2 %collective-permute-done.1 = bf16[256,1536]{1,0:T(8,128)(2,1)S(1)} collective-permute-done((bf16[256,1536]{1,0:T(8,128)(2,1)}, bf16[256,1536]{1,0:T(8,128)(2,1)S(1)}, u32[]{:S(2)}, u32[]{:S(2)}) %collective-permute-start.1) | collective-permute-done | bytes 786464 | tf_op jit(solution)/shard_map/ppermute | solution.py:30
  29.1 5.4 %multiply_convert_fusion = bf16[512,1536]{1,0:T(8,128)(2,1)} fusion(bf16[514,1536]{1,0:T(8,128)(2,1)S(1)} %constant_dynamic-update-slice_fusion, bf16[514,1536]{1,0:T(8,128)(2,1)S(1)} %pad_maximum_fusion.1, bf16[256,1536]{1,0:T(8,128)(2,1)S(1)} %copy-done.1, bf16[256,1536]{1,0:T(8,128)(2,1)S(1)} %collective-permute-done.1, f32[512]{0:T(512)S(1)} %get-tuple-element.16, ...), kind=kLoop, calls=%fused_computation.14 | loop fusion | flops 20447232 | bytes 9476096 | tf_op jit(solution)/shard_map/convert_element_type | solution.py:22
  34.5 54.3 %all-gather.2.cloned.1.call-done = bf16[1536,4608]{0,1:T(8,128)(2,1)} async-done(((bf16[1536,576]{0,1:T(8,128)(2,1)}), bf16[1536,4608]{0,1:T(8,128)(2,1)}) %all-gather.2.cloned.1.call-update) | async-done | bytes 14155792 | tf_op jit(solution)/shard_map/all_gather | solution.py:29
  88.8 9.1 %convolution_convert_fusion = bf16[256,4608]{1,0:T(8,128)(2,1)S(1)} fusion(bf16[1536,4608]{0,1:T(8,128)(2,1)} %all-gather.2.cloned.1.call-done, bf16[512,1536]{1,0:T(8,128)(2,1)} %multiply_convert_fusion), kind=kOutput, calls=%fused_computation.6 | convolution fusion | flops 3625058304 | bytes 17301504 | tf_op jit(solution)/shard_map/dot_general | solution.py:37
  98.1 2.0 copy-done.4
  100.2 6.4 %fusion.8 = bf16[256,3072]{1,0:T(8,128)(2,1)S(1)} fusion(bf16[1536,4608]{0,1:T(8,128)(2,1)} %all-gather.2.cloned.1.call-done, bf16[512,1536]{1,0:T(8,128)(2,1)S(1)} %copy-done.4), kind=kOutput, calls=%fused_computation.12 | convolution fusion | flops 2416705536 | bytes 11796480 | tf_op jit(solution)/shard_map/dot_general | solution.py:38
  106.6 1.9 pad_maximum_fusion
  108.5 4.8 %copy.16 = bf16[512,3072]{0,1:T(8,128)(2,1)} copy(bf16[512,3072]{1,0:T(8,128)(2,1)} %pad_maximum_fusion) | data formatting | bytes 6291456 | tf_op jit(solution)/shard_map/concatenate | solution.py:43
  113.5 2.7 fusion.11
  116.2 6.0 %fusion.24 = (f32[16,256]{1,0:T(8,128)S(1)}, f32[16,256,512]{2,1,0:T(8,128)}) fusion(f32[16,256,512]{2,1,0:T(8,128)S(1)} %fusion.11, pred[256,512]{1,0:T(8,128)(4,1)S(1)} %compare_and_fusion), kind=kOutput, calls=%fused_computation.48 | output fusion | flops 12583423 | bytes 16924672 | tf_op jit(solution)/shard_map/sub | solution.py:52
  122.3 4.9 %fusion.12 = bf16[16,96,256]{2,1,0:T(8,128)(2,1)S(1)} fusion(f32[16,256,512]{2,1,0:T(8,128)} %get-tuple-element.20, f32[16,256]{1,0:T(8,128)S(1)} %get-tuple-element.19, bf16[512,2,16,96]{0,3,2,1:T(8,128)(2,1)S(1)} %bitcast.23), kind=kOutput, calls=%fused_computation.20 | convolution fusion | flops 407240704 | bytes 10764288 | tf_op jit(solution)/shard_map/hqk,khv->qhv/dot_general | solution.py:54
  127.2 5.1 %fusion.25 = f32[1536,1536]{0,1:T(8,128)} fusion(bf16[256,1536]{0,1:T(8,128)(2,1)S(1)} %bitcast.25, bf16[256,1536]{1,0:T(8,128)(2,1)S(1)} %copy-done), kind=kOutput, calls=%fused_computation.49 | convolution fusion | flops 1207959552 | bytes 11010048 | tf_op jit(solution)/shard_map/dot_general | solution.py:57
  132.3 58.7 %reduce-scatter.5.cloned.1.call-done = f32[1536,192]{0,1:T(8,128)} async-done(((f32[1536,1536]{0,1:T(8,128)}), f32[1536,192]{0,1:T(8,128)}) %reduce-scatter.5.cloned.1.call-update) | async-done | bytes 1179664 | tf_op jit(solution)/shard_map/reduce_scatter | solution.py:60
  191.0 2.9 copy.19
  193.9 4.6 %convolution_convert_fusion.1 = bf16[256,1536]{1,0:T(8,128)(2,1)} fusion(bf16[256,1536]{0,1:T(8,128)(2,1)S(1)} %bitcast.26, bf16[1536,1536]{1,0:T(8,128)(2,1)} %param.12), kind=kOutput, calls=%fused_computation.15 | convolution fusion | flops 1208352768 | bytes 6291456 | tf_op jit(solution)/shard_map/dot_general | solution.py:56
  198.5 214.1 %reduce-scatter.7.cloned.1.call-done = f32[48,192]{1,0:T(8,128)} async-done(((f32[1536,192]{1,0:T(8,128)}), f32[48,192]{1,0:T(8,128)}) %reduce-scatter.7.cloned.1.call-update) | async-done | bytes 36880
  (29 shorter events, 2.2 us)
Async XLA Ops:
  7.2 120.0 %copy-start = (bf16[256,1536]{1,0:T(8,128)(2,1)S(1)}, bf16[256,1536]{1,0:T(8,128)(2,1)}, u32[]{:S(2)}) copy-start(bf16[256,1536]{1,0:T(8,128)(2,1)} %param.13) | copy-start | bytes 2359300
  7.2 21.4 %copy-start.1 = (bf16[256,1536]{1,0:T(8,128)(2,1)S(1)}, bf16[256,1536]{1,0:T(8,128)(2,1)}, u32[]{:S(2)}) copy-start(bf16[256,1536]{1,0:T(8,128)(2,1)} %param.7) | copy-start | bytes 2359300
  7.2 81.6 %all-gather.2.cloned.1.call-start = ((), (), s32[]{:S(2)}) async-start(), calls=%async_computation.2 | async-start | bytes 15925248 | tf_op jit(solution)/shard_map/all_gather | solution.py:29
  7.9 183.1 %reduce-scatter.5.cloned.1.call-start = ((), (), s32[]{:S(2)}) async-start(), calls=%async_computation.3 | async-start | bytes 10616832 | tf_op jit(solution)/shard_map/reduce_scatter | solution.py:60
  8.0 20.6 %collective-permute-start.1 = (bf16[256,1536]{1,0:T(8,128)(2,1)}, bf16[256,1536]{1,0:T(8,128)(2,1)S(1)}, u32[]{:S(2)}, u32[]{:S(2)}) collective-permute-start(bf16[256,1536]{1,0:T(8,128)(2,1)} %param.7), channel_id=1, source_target_pairs={{0,1},{1,2},{2,3},{3,4},{4,5},{5,6},{6,7},{7,8},{8,9},{9,10},{10,1... | collective-permute-start | bytes 2359304 | tf_op jit(solution)/shard_map/ppermute | solution.py:30
  12.2 16.5 %collective-permute-start = (bf16[2,1536]{1,0:T(2,128)(2,1)S(1)}, bf16[2,1536]{1,0:T(2,128)(2,1)S(1)}, u32[]{:S(2)}, u32[]{:S(2)}) collective-permute-start(bf16[2,1536]{1,0:T(2,128)(2,1)S(1)} %get-tuple-element.13), channel_id=1, source_target_pairs={{0,2},{1,3},{2,4},{3,5},{4,6},{5,7},{6,8},{7,9},{8,10},{9,11},{10,... | collective-permute-start | bytes 18440 | tf_op jit(solution)/shard_map/ppermute | solution.py:31
  16.8 11.8 %collective-permute-start.2 = (bf16[2,1536]{1,0:T(2,128)(2,1)S(1)}, bf16[2,1536]{1,0:T(2,128)(2,1)S(1)}, u32[]{:S(2)}, u32[]{:S(2)}) collective-permute-start(bf16[2,1536]{1,0:T(2,128)(2,1)S(1)} %get-tuple-element.14), channel_id=1, source_target_pairs={{1,0},{2,1},{3,2},{4,3},{5,4},{6,5},{7,6},{8,7},{9,8},{10,9},{11,1... | collective-permute-start | bytes 18440 | tf_op jit(solution)/shard_map/ppermute | solution.py:32
  97.9 8.7 %copy-start.3 = (bf16[256,4608]{1,0:T(8,128)(2,1)}, bf16[256,4608]{1,0:T(8,128)(2,1)S(1)}, u32[]{:S(2)}) copy-start(bf16[256,4608]{1,0:T(8,128)(2,1)S(1)} %convolution_convert_fusion) | copy-start | bytes 7077892
  97.9 2.3 copy-start.4
  108.5 4.8 %slice-start = ((bf16[256,4608]{1,0:T(8,128)(2,1)}), bf16[256,1536]{1,0:T(8,128)(2,1)S(1)}, s32[]{:S(2)}) async-start(bf16[256,4608]{1,0:T(8,128)(2,1)} %copy-done.3), calls=%async_computation.5 | async-start | bytes 1572864 | tf_op jit(solution)/shard_map/slice | solution.py:42
  116.2 6.0 %copy-start.2 = (bf16[512,3072]{0,1:T(8,128)(2,1)S(1)}, bf16[512,3072]{0,1:T(8,128)(2,1)}, u32[]{:S(2)}) copy-start(bf16[512,3072]{0,1:T(8,128)(2,1)} %copy.16) | copy-start | bytes 9437188
  132.3 280.4 %reduce-scatter.7.cloned.1.call-start = ((), (), s32[]{:S(2)}) async-start(), calls=%async_computation.4 | async-start | bytes 1622016
Sparse Core Ops, SparseCore 0:
  9.9 78.8 all-gather.1
  132.4 58.5 reduce-scatter.4
  195.4 217.2 reduce-scatter.6
where the time goes:
time: 420 us; the launch traced here: 419 us
  waiting for transfers between devices  334 us (80%)
  matrix products  32.8 us (8%)
  other arithmetic  15.8 us (4%)
  between operations  13.9 us (3%)
  local copies, waits for them, and re-layouts  13.1 us (3%)
  starting transfers between devices  9.47 us (2%)
    unnamed x4, waiting for transfers between devices  215 us
    reduce_scatter x1, waiting for transfers between devices, local(): lax.psum_scatter(grad_term, 'dp', scatter_dimension=1, tiled=True)  58.7 us
    all_gather x1, waiting for transfers between devices, local(): weights = lax.all_gather(w_qkv, 'dp', axis=1, tiled=True)  54.3 us
    dot_general x1, matrix products, local(): jnp.dot(activ[rows:], weights, preferred_element_type=jnp.float32)  9.13 us
  transfers between devices with their start and end apart: 6, of which 4 were waited for; matrix products, arithmetic and copies ran while one was open for 4% of the time, Pallas kernels for 0%

commit v1 on v0

--- a/solution.py
+++ b/solution.py
@@ -3,6 +3,7 @@
 import jax.numpy as jnp
 from jax import lax
 from jax.sharding import PartitionSpec as P
+from jax.lax import axis_index, axis_size, ppermute
 
 KER = 5
 HEADS = 16
@@ -26,7 +27,19 @@
     rows, width = frames.shape
     count = lax.axis_size("tm")
     me = lax.axis_index("tm")
-    weights = lax.all_gather(w_qkv, "dp", axis=1, tiled=True)
+    degree = axis_size("dp")
+    parts_seen = [(pp, (pp + 1) % degree) for pp in range(degree)]
+    windows = [(pp, (pp - 1) % degree) for pp in range(degree)]
+    long_array, side_arr = ([w_qkv], [w_qkv])
+    for _ in range(degree // 2):
+        later = ppermute(long_array[-1], "dp", parts_seen)
+        long_array.append(later)
+    k = 0
+    while k < (degree - 1) // 2:
+        side_arr.append(ppermute(side_arr[-1], "dp", windows))
+        k += 1
+    item_now = jnp.concatenate([*long_array[::-1], *side_arr[1:]], axis=1)
+    weights = jnp.roll(item_now, (axis_index("dp") - degree // 2) * w_qkv.shape[1], axis=1)
     before = lax.ppermute(frames, "tm", [(i, i + 1) for i in range(count - 1)])
     far = lax.ppermute(frames[-HALF:], "tm", [(i, i + 2) for i in range(count - 2)])
     after = lax.ppermute(frames[:HALF], "tm", [(i + 1, i) for i in range(count - 1)])

time: 420 us -> 482 us (1.15)
  local copies, waits for them, and re-layouts: 13.1 us -> 47.3 us
  waiting for transfers between devices: 334 us -> 346 us
  matrix products: 32.8 us -> 40 us
  starting transfers between devices: 9.47 us -> 15.6 us
    ppermute x0 -> x7, waiting for transfers between devices: none -> 60.8 us  [the longest x4 42.5 us: local(): later = ppermute(long_array[-1], 'dp', parts_seen)]
    all_gather x1 -> x0, waiting for transfers between devices: 54.3 us -> none  [local(): weights = lax.all_gather(w_qkv, 'dp', axis=1, tiled=True)]
    unnamed x13 -> x30, local copies, waits for them, and re-layouts: 5.07 us -> 34.5 us
    reduce_scatter x1, waiting for transfers between devices: 58.7 us -> 66.5 us  [local(): lax.psum_scatter(grad_term, 'dp', scatter_dimension=1, tiled=True)]
    dot_general x1, matrix products: 9.13 us -> 16.1 us  [local(): jnp.dot(activ[rows:], weights, preferred_element_type=jnp.float32)]
    unnamed x4 -> x3, waiting for transfers between devices: 215 us -> 214 us
  transfers between devices with their start and end apart: 6 -> 12, of which waited for: 4 -> 7; matrix products, arithmetic and copies ran while one was open for 4% -> 7% of each run, Pallas kernels for 0% -> 0%
where the time goes in v1:
time: 482 us; the launch traced here: 481 us
  waiting for transfers between devices  346 us (72%)
  local copies, waits for them, and re-layouts  47.3 us (10%)
  matrix products  40 us (8%)
  other arithmetic  17.1 us (4%)
  starting transfers between devices  15.6 us (3%)
  between operations  14.2 us (3%)
    unnamed x3, waiting for transfers between devices  214 us
    reduce_scatter x1, waiting for transfers between devices, local(): lax.psum_scatter(grad_term, 'dp', scatter_dimension=1, tiled=True)  66.5 us
    ppermute x4, waiting for transfers between devices, local(): later = ppermute(long_array[-1], 'dp', parts_seen)  42.5 us
    unnamed x30, local copies, waits for them, and re-layouts  34.5 us
    ppermute x3, waiting for transfers between devices, local(): side_arr.append(ppermute(side_arr[-1], 'dp', windows))  18.3 us
    dot_general x1, matrix products, local(): jnp.dot(activ[rows:], weights, preferred_element_type=jnp.float32)  16.1 us
  transfers between devices with their start and end apart: 12, of which 7 were waited for; matrix products, arithmetic and copies ran while one was open for 7% of the time, Pallas kernels for 0%

profile of v1, /device:TPU:8, one launch (start us, length us, event | category | flops | bytes accessed | tf_op | source)
XLA Modules:
  0.0 480.7 jit_solution(7508311710948390545)
XLA Ops:
  7.3 22.1 %collective-permute-done.3 = bf16[1536,576]{0,1:T(8,128)(2,1)S(1)} collective-permute-done((bf16[1536,576]{0,1:T(8,128)(2,1)}, bf16[1536,576]{0,1:T(8,128)(2,1)S(1)}, u32[]{:S(2)}, u32[]{:S(2)}) %collective-permute-start.3) | collective-permute-done | bytes 1769504 | tf_op jit(solution)/shard_map/ppermute | solution.py:35
  31.2 20.3 %collective-permute-done.4 = bf16[1536,576]{0,1:T(8,128)(2,1)} collective-permute-done((bf16[1536,576]{0,1:T(8,128)(2,1)S(1)}, bf16[1536,576]{0,1:T(8,128)(2,1)}, u32[]{:S(2)}, u32[]{:S(2)}) %collective-permute-start.4) | collective-permute-done | bytes 1769504 | tf_op jit(solution)/shard_map/ppermute | solution.py:35
  51.5 4.3 collective-permute-start.1
  57.8 5.2 %collective-permute-start = (bf16[2,1536]{1,0:T(2,128)(2,1)S(1)}, bf16[2,1536]{1,0:T(2,128)(2,1)S(1)}, u32[]{:S(2)}, u32[]{:S(2)}) collective-permute-start(bf16[2,1536]{1,0:T(2,128)(2,1)S(1)} %get-tuple-element.13), channel_id=1, source_target_pairs={{0,2},{1,3},{2,4},{3,5},{4,6},{5,7},{6,8},{7,9},{8,10},{9,11},{10,... | collective-permute-start | bytes 18440 | tf_op jit(solution)/shard_map/ppermute | solution.py:44
  67.2 5.2 %collective-permute-done.1 = bf16[256,1536]{1,0:T(8,128)(2,1)} collective-permute-done((bf16[256,1536]{1,0:T(8,128)(2,1)}, bf16[256,1536]{1,0:T(8,128)(2,1)}, u32[]{:S(2)}, u32[]{:S(2)}) %collective-permute-start.1) | collective-permute-done | bytes 786464 | tf_op jit(solution)/shard_map/ppermute | solution.py:43
  77.3 5.6 %multiply_convert_fusion = bf16[512,1536]{1,0:T(8,128)(2,1)S(1)} fusion(bf16[514,1536]{1,0:T(8,128)(2,1)S(1)} %constant_dynamic-update-slice_fusion, bf16[514,1536]{1,0:T(8,128)(2,1)S(1)} %pad_maximum_fusion.1, bf16[256,1536]{1,0:T(8,128)(2,1)S(1)} %copy-done.1, bf16[256,1536]{1,0:T(8,128)(2,1)} %collective-permute-done.1, f32[512]{0:T(512)S(1)} %get-tuple-element.16, ...), kind=kLoop, calls=%fused_computation.16 | loop fusion | flops 20447232 | bytes 9476096 | tf_op jit(solution)/shard_map/convert_element_type | solution.py:23
  82.9 12.3 %collective-permute-done.8 = bf16[1536,576]{0,1:T(8,128)(2,1)S(1)} collective-permute-done((bf16[1536,576]{0,1:T(8,128)(2,1)}, bf16[1536,576]{0,1:T(8,128)(2,1)S(1)}, u32[]{:S(2)}, u32[]{:S(2)}) %collective-permute-start.8) | collective-permute-done | bytes 1769504 | tf_op jit(solution)/shard_map/ppermute | solution.py:39
  98.6 2.8 constant_dynamic-update-slice_fusion.17
  101.4 3.0 constant_dynamic-update-slice_fusion.16
  107.1 2.8 constant_dynamic-update-slice_fusion.13
  111.3 6.0 %collective-permute-done.9 = bf16[1536,576]{0,1:T(8,128)(2,1)S(1)} collective-permute-done((bf16[1536,576]{0,1:T(8,128)(2,1)S(1)}, bf16[1536,576]{0,1:T(8,128)(2,1)S(1)}, u32[]{:S(2)}, u32[]{:S(2)}) %collective-permute-start.9) | collective-permute-done | bytes 1769504 | tf_op jit(solution)/shard_map/ppermute | solution.py:39
  120.0 2.8 constant_dynamic-update-slice_fusion.9
  122.8 2.8 constant_dynamic-update-slice_fusion.8
  128.3 2.8 constant_dynamic-update-slice_fusion.5
  133.9 16.1 %fusion.5 = bf16[256,4608]{1,0:T(8,128)(2,1)} fusion(bf16[1536,9216]{0,1:T(8,128)(2,1)} %constant_dynamic-update-slice_fusion.3, s32[]{:T(128)S(6)} %select_n.25, bf16[512,1536]{1,0:T(8,128)(2,1)S(1)} %multiply_convert_fusion), kind=kOutput, calls=%fused_computation.8 | convolution fusion | flops 3625058304 | bytes 17301508 | tf_op jit(solution)/shard_map/dot_general | solution.py:50
  153.8 6.6 %fusion.13 = bf16[256,3072]{1,0:T(8,128)(2,1)S(1)} fusion(bf16[1536,9216]{0,1:T(8,128)(2,1)} %constant_dynamic-update-slice_fusion.3, s32[]{:T(128)S(6)} %add.53, bf16[512,1536]{1,0:T(8,128)(2,1)} %copy-done.5), kind=kOutput, calls=%fused_computation.14 | convolution fusion | flops 2416705536 | bytes 11796484 | tf_op jit(solution)/shard_map/dot_general | solution.py:51
  162.3 4.8 copy.16
  169.8 6.0 %fusion.31 = (f32[16,256]{1,0:T(8,128)S(1)}, f32[16,256,512]{2,1,0:T(8,128)}) fusion(f32[16,256,512]{2,1,0:T(8,128)S(1)} %fusion.16, pred[256,512]{1,0:T(8,128)(4,1)S(1)} %compare_and_fusion), kind=kOutput, calls=%fused_computation.68 | output fusion | flops 12583423 | bytes 16924672 | tf_op jit(solution)/shard_map/sub | solution.py:65
  175.8 4.9 %fusion.17 = bf16[16,96,256]{2,1,0:T(8,128)(2,1)S(1)} fusion(f32[16,256,512]{2,1,0:T(8,128)} %get-tuple-element.20, f32[16,256]{1,0:T(8,128)S(1)} %get-tuple-element.19, bf16[512,2,16,96]{0,3,2,1:T(8,128)(2,1)S(1)} %bitcast.22), kind=kOutput, calls=%fused_computation.22 | convolution fusion | flops 407240704 | bytes 10764288 | tf_op jit(solution)/shard_map/hqk,khv->qhv/dot_general | solution.py:67
  180.7 5.1 %fusion.32 = f32[1536,1536]{0,1:T(8,128)} fusion(bf16[256,1536]{0,1:T(8,128)(2,1)S(1)} %bitcast.24, bf16[256,1536]{1,0:T(8,128)(2,1)S(1)} %copy-done), kind=kOutput, calls=%fused_computation.69 | convolution fusion | flops 1207959552 | bytes 11010048 | tf_op jit(solution)/shard_map/dot_general | solution.py:70
  185.9 66.5 %reduce-scatter.5.cloned.1.call-done = f32[1536,192]{0,1:T(8,128)} async-done(((f32[1536,1536]{0,1:T(8,128)}), f32[1536,192]{0,1:T(8,128)}) %reduce-scatter.5.cloned.1.call-update) | async-done | bytes 1179664 | tf_op jit(solution)/shard_map/reduce_scatter | solution.py:73
  252.4 2.9 copy.19
  255.3 4.6 convolution_convert_fusion
  259.9 213.9 %reduce-scatter.7.cloned.1.call-done = f32[48,192]{1,0:T(8,128)} async-done(((f32[1536,192]{1,0:T(8,128)}), f32[48,192]{1,0:T(8,128)}) %reduce-scatter.7.cloned.1.call-update) | async-done | bytes 36880
  (57 shorter events, 37.0 us)
Async XLA Ops:
  7.2 173.5 %copy-start = (bf16[256,1536]{1,0:T(8,128)(2,1)S(1)}, bf16[256,1536]{1,0:T(8,128)(2,1)}, u32[]{:S(2)}) copy-start(bf16[256,1536]{1,0:T(8,128)(2,1)} %param.13) | copy-start | bytes 2359300
  7.2 68.6 %copy-start.1 = (bf16[256,1536]{1,0:T(8,128)(2,1)S(1)}, bf16[256,1536]{1,0:T(8,128)(2,1)}, u32[]{:S(2)}) copy-start(bf16[256,1536]{1,0:T(8,128)(2,1)} %param.7) | copy-start | bytes 2359300
  7.2 245.2 %reduce-scatter.5.cloned.1.call-start = ((), (), s32[]{:S(2)}) async-start(), calls=%async_computation.2 | async-start | bytes 10616832 | tf_op jit(solution)/shard_map/reduce_scatter | solution.py:73
  7.2 22.2 %collective-permute-start.3 = (bf16[1536,576]{0,1:T(8,128)(2,1)}, bf16[1536,576]{0,1:T(8,128)(2,1)S(1)}, u32[]{:S(2)}, u32[]{:S(2)}) collective-permute-start(bf16[1536,576]{0,1:T(8,128)(2,1)} %param.11), channel_id=1, source_target_pairs={{0,32},{32,64},{64,96},{96,128},{128,160},{160,192},{192,224},{224... | collective-permute-start | bytes 5308424 | tf_op jit(solution)/shard_map/ppermute | solution.py:35
  29.4 22.1 %collective-permute-start.4 = (bf16[1536,576]{0,1:T(8,128)(2,1)S(1)}, bf16[1536,576]{0,1:T(8,128)(2,1)}, u32[]{:S(2)}, u32[]{:S(2)}) collective-permute-start(bf16[1536,576]{0,1:T(8,128)(2,1)S(1)} %collective-permute-done.3), channel_id=1, source_target_pairs={{0,32},{32,64},{64,96},{96,128},{128,160},{160,192},{192,224},{224... | collective-permute-start | bytes 5308424 | tf_op jit(solution)/shard_map/ppermute | solution.py:35
  29.4 45.4 %collective-permute-start.7 = (bf16[1536,576]{0,1:T(8,128)(2,1)}, bf16[1536,576]{0,1:T(8,128)(2,1)}, u32[]{:S(2)}, u32[]{:S(2)}) collective-permute-start(bf16[1536,576]{0,1:T(8,128)(2,1)} %param.11), channel_id=1, source_target_pairs={{0,224},{32,0},{64,32},{96,64},{128,96},{160,128},{192,160},{224,1... | collective-permute-start | bytes 5308424 | tf_op jit(solution)/shard_map/ppermute | solution.py:39
  51.5 23.4 %collective-permute-start.5 = (bf16[1536,576]{0,1:T(8,128)(2,1)}, bf16[1536,576]{0,1:T(8,128)(2,1)}, u32[]{:S(2)}, u32[]{:S(2)}) collective-permute-start(bf16[1536,576]{0,1:T(8,128)(2,1)} %collective-permute-done.4), channel_id=1, source_target_pairs={{0,32},{32,64},{64,96},{96,128},{128,160},{160,192},{192,224},{224... | collective-permute-start | bytes 5308424 | tf_op jit(solution)/shard_map/ppermute | solution.py:35
  51.5 21.0 %collective-permute-start.1 = (bf16[256,1536]{1,0:T(8,128)(2,1)}, bf16[256,1536]{1,0:T(8,128)(2,1)}, u32[]{:S(2)}, u32[]{:S(2)}) collective-permute-start(bf16[256,1536]{1,0:T(8,128)(2,1)} %param.7), channel_id=1, source_target_pairs={{0,1},{1,2},{2,3},{3,4},{4,5},{5,6},{6,7},{7,8},{8,9},{9,10},{10,1... | collective-permute-start | bytes 2359304 | tf_op jit(solution)/shard_map/ppermute | solution.py:43
  56.5 19.2 %collective-permute-start.2 = (bf16[2,1536]{1,0:T(2,128)(2,1)S(1)}, bf16[2,1536]{1,0:T(2,128)(2,1)S(1)}, u32[]{:S(2)}, u32[]{:S(2)}) collective-permute-start(bf16[2,1536]{1,0:T(2,128)(2,1)S(1)} %get-tuple-element.14), channel_id=1, source_target_pairs={{1,0},{2,1},{3,2},{4,3},{5,4},{6,5},{7,6},{8,7},{9,8},{10,9},{11,1... | collective-permute-start | bytes 18440 | tf_op jit(solution)/shard_map/ppermute | solution.py:45
  57.8 17.9 %collective-permute-start = (bf16[2,1536]{1,0:T(2,128)(2,1)S(1)}, bf16[2,1536]{1,0:T(2,128)(2,1)S(1)}, u32[]{:S(2)}, u32[]{:S(2)}) collective-permute-start(bf16[2,1536]{1,0:T(2,128)(2,1)S(1)} %get-tuple-element.13), channel_id=1, source_target_pairs={{0,2},{1,3},{2,4},{3,5},{4,6},{5,7},{6,8},{7,9},{8,10},{9,11},{10,... | collective-permute-start | bytes 18440 | tf_op jit(solution)/shard_map/ppermute | solution.py:44
  74.8 20.4 %collective-permute-start.8 = (bf16[1536,576]{0,1:T(8,128)(2,1)}, bf16[1536,576]{0,1:T(8,128)(2,1)S(1)}, u32[]{:S(2)}, u32[]{:S(2)}) collective-permute-start(bf16[1536,576]{0,1:T(8,128)(2,1)} %collective-permute-done.7), channel_id=1, source_target_pairs={{0,224},{32,0},{64,32},{96,64},{128,96},{160,128},{192,160},{224,1... | collective-permute-start | bytes 5308424 | tf_op jit(solution)/shard_map/ppermute | solution.py:39
  74.8 22.4 %collective-permute-start.6 = (bf16[1536,576]{0,1:T(8,128)(2,1)}, bf16[1536,576]{0,1:T(8,128)(2,1)S(1)}, u32[]{:S(2)}, u32[]{:S(2)}) collective-permute-start(bf16[1536,576]{0,1:T(8,128)(2,1)} %collective-permute-done.5), channel_id=1, source_target_pairs={{0,32},{32,64},{64,96},{96,128},{128,160},{160,192},{192,224},{224... | collective-permute-start | bytes 5308424 | tf_op jit(solution)/shard_map/ppermute | solution.py:35
  82.9 51.0 %copy-start.5 = (bf16[512,1536]{1,0:T(8,128)(2,1)}, bf16[512,1536]{1,0:T(8,128)(2,1)S(1)}, u32[]{:S(2)}) copy-start(bf16[512,1536]{1,0:T(8,128)(2,1)S(1)} %multiply_convert_fusion) | copy-start | bytes 4718596
  95.2 22.1 %collective-permute-start.9 = (bf16[1536,576]{0,1:T(8,128)(2,1)S(1)}, bf16[1536,576]{0,1:T(8,128)(2,1)S(1)}, u32[]{:S(2)}, u32[]{:S(2)}) collective-permute-start(bf16[1536,576]{0,1:T(8,128)(2,1)S(1)} %collective-permute-done.8), channel_id=1, source_target_pairs={{0,224},{32,0},{64,32},{96,64},{128,96},{160,128},{192,160},{224,1... | collective-permute-start | bytes 5308424 | tf_op jit(solution)/shard_map/ppermute | solution.py:39
  101.4 4.3 copy-start.2
  162.3 4.8 copy-start.4
  169.8 6.0 %copy-start.3 = (bf16[512,3072]{0,1:T(8,128)(2,1)S(1)}, bf16[512,3072]{0,1:T(8,128)(2,1)}, u32[]{:S(2)}) copy-start(bf16[512,3072]{0,1:T(8,128)(2,1)} %copy.16) | copy-start | bytes 9437188
  185.8 288.1 %reduce-scatter.7.cloned.1.call-start = ((), (), s32[]{:S(2)}) async-start(), calls=%async_computation.3 | async-start | bytes 1622016
Sparse Core Ops, SparseCore 0:
  185.9 66.4 reduce-scatter.4
  256.8 217.0 reduce-scatter.6
